TPU v7x, 128 devices: a whole 4x4x4 slice. The times are simulated.
128 devices in a mesh: subj: 4 (over z_lo, core), blk: 32 (over y, x, z_hi).
Axes of the slice: x: 4, y: 4, z: 4 (z_hi: 2, z_lo: 2; z = z_hi * 2 + z_lo), core: 2. Of those that a mesh axis runs over, the one named last changes fastest.
Arguments:
- series: bfloat16 [8, 1200, 32768], P('subj', None, 'blk'), may hold values from -170 to 170
- circle_step: int32 [1], replicated, may hold values from 1 to 31
- vertex_count: int32 [32], replicated, may hold values from 1 to 1024, 28672 in all
Outputs:
- group_z: float32 [1024, 32768], P('subj', 'blk')
Inputs may be any that keep to these rules, and one draw needn't show every extreme that they name: `vertex_count`: the counts sum to 28672.
All inputs are finite; a program needn't handle non-finite values.
Results may differ from a plain program's by a relative error of at most 0.0019.
Values may be sent and summed in bfloat16 or wider, within the bound.
No kernel may reach another device: no remote copies, remote signals or barrier semaphores. Data moves between devices by JAX's collectives and lax.ppermute only.
A program may use at most 192 MiB of HBM per device.

v0:
```python
import math

import jax
import jax.numpy as jnp
from jax import lax
from jax.sharding import PartitionSpec as P

tr_seconds = 0.72
low_cut = 0.01
high_cut = 0.08
shrink = 0.98
epsilon = 1e-06


def shifted(value, axis, steps):
    count = lax.axis_size(axis)
    pairs = [(source, (source + steps) % count) for source in range(count)]
    return lax.ppermute(value, axis, pairs)


def tables(frames):
    index_row = jnp.arange(frames, dtype=jnp.int32)
    product_index = (2 * index_row[None, :] + 1) * index_row[:, None] % (4 * frames)
    phase_angle = product_index.astype(jnp.float32) * (math.pi / (2 * frames))
    row_scale = jnp.where(index_row == 0, math.sqrt(0.5), 1.0).astype(jnp.float32)
    cosine_table = jnp.cos(phase_angle) * math.sqrt(2.0 / frames) * row_scale[:, None]
    frequency = index_row.astype(jnp.float32) / (2 * frames * tr_seconds)
    high_pass = frequency / low_cut / jnp.sqrt(1.0 + (frequency / low_cut) ** 2)
    low_pass = 1.0 / jnp.sqrt(1.0 + (frequency / high_cut) ** 2)
    return (cosine_table.astype(jnp.bfloat16), (high_pass * low_pass)[:, None])


def normalize(raw_block, cosine_table, gains):
    coefficients = jnp.dot(cosine_table, raw_block, preferred_element_type=jnp.float32)
    weighted = (coefficients * gains).astype(jnp.bfloat16)
    filtered = jnp.dot(cosine_table.T, weighted, preferred_element_type=jnp.float32)
    frame_mean = jnp.mean(filtered, axis=0, keepdims=True)
    centered = filtered - frame_mean
    variance = jnp.mean(centered * centered, axis=0, keepdims=True)
    return (centered * lax.rsqrt(variance + epsilon)).astype(jnp.bfloat16)


def normalize_all(series, cosine_table, gains):
    return jnp.stack(
        [normalize(series[subject], cosine_table, gains) for subject in range(series.shape[0])]
    )


def fisher(correlation):
    scaled = shrink * correlation
    return 0.5 * (jnp.log(1.0 + scaled) - jnp.log(1.0 - scaled))


def local(series, circle_step, vertex_count):
    subj_local, frames, width = series.shape
    cosine_table, gains = tables(frames)
    shift_count = circle_step[0]
    block_total = lax.axis_size("blk")
    own_block = lax.axis_index("blk")
    partner = (own_block - shift_count) % block_total
    bit_count = (block_total - 1).bit_length()
    own_z = normalize_all(series, cosine_table, gains)
    payload = own_z
    for bit_pos in range(bit_count):
        moved = shifted(payload, "blk", 1 << bit_pos)
        use_moved = shift_count >> bit_pos & 1 == 1
        payload = jnp.where(use_moved, moved, payload)
    subj_total = lax.axis_size("subj")
    subj_index = lax.axis_index("subj")
    row_share = width // subj_total
    running = jnp.zeros((row_share * lax.axis_size("subj"), width), jnp.float32)
    for subject in range(subj_local):
        slice_rows = payload[subject]
        correlation = (
            lax.dot_general(
                slice_rows,
                own_z[subject],
                (((0,), (0,)), ((), ())),
                preferred_element_type=jnp.float32,
            )
            / frames
        )
        running = running + fisher(correlation)
    summed = lax.psum_scatter(running, "subj", scatter_dimension=0, tiled=True)
    block_ids = jnp.arange(block_total, dtype=jnp.int32)
    own_count = jnp.sum(jnp.where(block_ids == own_block, vertex_count, 0))
    partner_count = jnp.sum(jnp.where(block_ids == partner, vertex_count, 0))
    row_slots = subj_index * row_share + jnp.arange(row_share, dtype=jnp.int32)
    col_slots = jnp.arange(width, dtype=jnp.int32)
    keep_mask = (row_slots < partner_count)[:, None] & (col_slots < own_count)[None, :]
    return jnp.where(keep_mask, summed / (subj_local * subj_total), 0.0)


def solution(mesh):
    in_specs = (P("subj", None, "blk"), P(), P())
    out_specs = P("subj", "blk")
    return jax.shard_map(local, mesh=mesh, in_specs=in_specs, out_specs=out_specs, check_vma=False)
```

profile of v0, /device:TPU:1, one launch (start us, length us, event | category | flops | bytes accessed | tf_op | source)
XLA Modules:
  0.0 773.0 jit_solution(1398568418470547376)
XLA Ops:
  6.5 0.0 reduce-scatter.2.cloned.1.call-start
  6.6 23.6 %fusion.12.clone.5 = bf16[1200,1200]{1,0:T(8,128)(2,1)S(1)} fusion(f32[1200]{0:T(1024)S(1)} %get-tuple-element.12, s32[1200]{0:T(1024)S(1)} %multiply_add_fusion), kind=kLoop, calls=%fused_computation.5.clone.2.clone.clone.clone.2 | loop fusion | flops 15840000 | bytes 2889600 | tf_op jit(solution)/shard_map/reduce_sum | solution.py:37
  30.2 24.6 %fusion.9.clone.5 = bf16[1200,1200]{1,0:T(8,128)(2,1)} fusion(f32[1200]{0:T(1024)S(1)} %get-tuple-element.12, s32[1200]{0:T(1024)S(1)} %multiply_add_fusion), kind=kLoop, calls=%fused_computation.5.clone.clone.clone.clone.2 | loop fusion | flops 15840000 | bytes 2889600 | tf_op jit(solution)/shard_map/reduce_sum | solution.py:37
  54.8 35.4 %fusion.49 = (f32[1024]{0:T(1024)S(1)}, f32[1200,1024]{1,0:T(8,128)}) fusion(f32[1200]{0:T(1024)S(1)} %get-tuple-element.12, s32[1200]{0:T(1024)S(1)} %multiply_add_fusion, f32[1200]{0:T(1024)S(1)} %get-tuple-element.11, bf16[2,1200,1024]{2,1,0:T(8,128)(2,1)} %param.3, bf16[1200,1200]{1,0:T(8,128)(2,1)S(1)} %fusion.12.clone.5), kind=kOutput, calls=%fused_computation.57 | convolution fusion | flops 5917765632 | bytes 10271296 | tf_op jit(solution)/shard_map/dot_general | solution.py:36
  90.3 0.0 copy-start.1
  90.3 3.1 multiply_reduce_fusion.1
  93.4 0.8 copy-done.1
  94.1 0.7 fusion.28
  94.9 35.8 %fusion.44 = (f32[1024]{0:T(1024)S(1)}, f32[1200,1024]{1,0:T(8,128)}) fusion(f32[1200]{0:T(1024)S(1)} %get-tuple-element.12, s32[1200]{0:T(1024)S(1)} %multiply_add_fusion, bf16[2,1200,1024]{2,1,0:T(8,128)(2,1)} %param.3, f32[1200]{0:T(1024)S(1)} %get-tuple-element.11, bf16[1200,1200]{1,0:T(8,128)(2,1)} %fusion.9.clone.5), kind=kOutput, calls=%fused_computation.56 | convolution fusion | flops 5917765632 | bytes 10463296 | tf_op jit(solution)/shard_map/dot_general | solution.py:36
  130.6 0.0 copy-start.2
  130.7 3.1 multiply_reduce_fusion
  133.8 0.7 copy-done.2
  134.5 0.8 fusion.29
  135.3 0.0 copy-start
  135.3 2.9 pad_maximum_fusion
  138.1 4.4 collective-permute-start
  143.2 0.0 copy-done
  143.2 110.0 %collective-permute-done = bf16[2,1200,1024]{2,1,0:T(8,128)(2,1)} collective-permute-done((bf16[2,1200,1024]{2,1,0:T(8,128)(2,1)}, bf16[2,1200,1024]{2,1,0:T(8,128)(2,1)}, u32[]{:S(2)}, u32[]{:S(2)}) %collective-permute-start) | collective-permute-done | bytes 4915232 | tf_op jit(solution)/shard_map/ppermute | solution.py:18
  253.3 6.0 broadcast_select_fusion
  259.3 0.0 collective-permute-start.1
  259.3 109.9 %collective-permute-done.1 = bf16[2,1200,1024]{2,1,0:T(8,128)(2,1)} collective-permute-done((bf16[2,1200,1024]{2,1,0:T(8,128)(2,1)}, bf16[2,1200,1024]{2,1,0:T(8,128)(2,1)}, u32[]{:S(2)}, u32[]{:S(2)}) %collective-permute-start.1) | collective-permute-done | bytes 4915232 | tf_op jit(solution)/shard_map/ppermute | solution.py:18
  369.2 7.3 broadcast_select_fusion.1
  376.5 0.0 collective-permute-start.2
  376.5 109.3 %collective-permute-done.2 = bf16[2,1200,1024]{2,1,0:T(8,128)(2,1)} collective-permute-done((bf16[2,1200,1024]{2,1,0:T(8,128)(2,1)}, bf16[2,1200,1024]{2,1,0:T(8,128)(2,1)}, u32[]{:S(2)}, u32[]{:S(2)}) %collective-permute-start.2) | collective-permute-done | bytes 4915232 | tf_op jit(solution)/shard_map/ppermute | solution.py:18
  485.8 5.1 broadcast_select_fusion.2
  490.9 0.0 collective-permute-start.3
  490.9 106.0 %collective-permute-done.3 = bf16[2,1200,1024]{2,1,0:T(8,128)(2,1)} collective-permute-done((bf16[2,1200,1024]{2,1,0:T(8,128)(2,1)}, bf16[2,1200,1024]{2,1,0:T(8,128)(2,1)}, u32[]{:S(2)}, u32[]{:S(2)}) %collective-permute-start.3) | collective-permute-done | bytes 4915232 | tf_op jit(solution)/shard_map/ppermute | solution.py:18
  596.8 5.1 broadcast_select_fusion.3
  601.9 0.0 collective-permute-start.4
  601.9 0.0 slice-start
  601.9 0.0 slice-start.1
  601.9 105.3 %collective-permute-done.4 = bf16[2,1200,1024]{2,1,0:T(8,128)(2,1)} collective-permute-done((bf16[2,1200,1024]{2,1,0:T(8,128)(2,1)}, bf16[2,1200,1024]{2,1,0:T(8,128)(2,1)}, u32[]{:S(2)}, u32[]{:S(2)}) %collective-permute-start.4) | collective-permute-done | bytes 4915232 | tf_op jit(solution)/shard_map/ppermute | solution.py:18
  707.2 3.0 broadcast_select_fusion.4
  710.2 0.0 slice-done
  710.2 0.0 slice-done.1
  710.2 0.0 slice-start.3
  710.3 3.1 fusion.15
  713.3 0.0 slice-done.2
  713.3 0.0 slice-done.3
  713.3 0.0 copy-start.3
  713.4 6.3 add_multiply_fusion
  719.7 0.0 reduce-scatter.2.cloned.1.call-update
  719.7 0.0 copy-done.3
  719.8 0.7 fusion.30
  720.4 0.7 add_compare_fusion
  721.1 0.6 iota_compare_fusion.1
  721.7 41.8 %reduce-scatter.2.cloned.1.call-done = f32[256,1024]{1,0:T(8,128)} async-done(((f32[1024,1024]{1,0:T(8,128)}), f32[256,1024]{1,0:T(8,128)}) %reduce-scatter.2.cloned.1.call-update) | async-done | bytes 1048592 | tf_op jit(solution)/shard_map/reduce_scatter | solution.py:84
  763.5 2.4 multiply_select_fusion
  (9 shorter events, 0.0 us)
Async XLA Ops:
  6.5 757.0 %reduce-scatter.2.cloned.1.call-start = ((), (), s32[]{:S(2)}) async-start(), calls=%async_computation.1 | async-start | bytes 5242880 | tf_op jit(solution)/shard_map/reduce_scatter | solution.py:84
  90.3 3.9 copy-start.1
  130.6 3.9 copy-start.2
  135.3 7.9 %copy-start = (bf16[1,1200,1024]{2,1,0:T(8,128)(2,1)}, bf16[1,1200,1024]{2,1,0:T(8,128)(2,1)S(1)}, u32[]{:S(2)}) copy-start(bf16[1,1200,1024]{2,1,0:T(8,128)(2,1)S(1)} %fusion.29) | copy-start | bytes 7372804
  138.1 115.1 %collective-permute-start = (bf16[2,1200,1024]{2,1,0:T(8,128)(2,1)}, bf16[2,1200,1024]{2,1,0:T(8,128)(2,1)}, u32[]{:S(2)}, u32[]{:S(2)}) collective-permute-start(bf16[2,1200,1024]{2,1,0:T(8,128)(2,1)} %pad_maximum_fusion), channel_id=1, source_target_pairs={{0,1},{1,2},{2,3},{3,4},{4,5},{5,6},{6,7},{7,8},{8,9},{9,10},{10,1... | collective-permute-start | bytes 14745608 | tf_op jit(solution)/shard_map/ppermute | solution.py:18
  259.3 109.9 %collective-permute-start.1 = (bf16[2,1200,1024]{2,1,0:T(8,128)(2,1)}, bf16[2,1200,1024]{2,1,0:T(8,128)(2,1)}, u32[]{:S(2)}, u32[]{:S(2)}) collective-permute-start(bf16[2,1200,1024]{2,1,0:T(8,128)(2,1)} %broadcast_select_fusion), channel_id=1, source_target_pairs={{0,2},{1,3},{2,4},{3,5},{4,6},{5,7},{6,8},{7,9},{8,10},{9,11},{10,... | collective-permute-start | bytes 14745608 | tf_op jit(solution)/shard_map/ppermute | solution.py:18
  376.5 109.3 %collective-permute-start.2 = (bf16[2,1200,1024]{2,1,0:T(8,128)(2,1)}, bf16[2,1200,1024]{2,1,0:T(8,128)(2,1)}, u32[]{:S(2)}, u32[]{:S(2)}) collective-permute-start(bf16[2,1200,1024]{2,1,0:T(8,128)(2,1)} %broadcast_select_fusion.1), channel_id=1, source_target_pairs={{0,4},{1,5},{2,6},{3,7},{4,8},{5,9},{6,10},{7,11},{8,12},{9,13},{1... | collective-permute-start | bytes 14745608 | tf_op jit(solution)/shard_map/ppermute | solution.py:18
  490.9 106.0 %collective-permute-start.3 = (bf16[2,1200,1024]{2,1,0:T(8,128)(2,1)}, bf16[2,1200,1024]{2,1,0:T(8,128)(2,1)}, u32[]{:S(2)}, u32[]{:S(2)}) collective-permute-start(bf16[2,1200,1024]{2,1,0:T(8,128)(2,1)} %broadcast_select_fusion.2), channel_id=1, source_target_pairs={{0,8},{1,9},{2,10},{3,11},{4,12},{5,13},{6,14},{7,15},{8,16},{9,17... | collective-permute-start | bytes 14745608 | tf_op jit(solution)/shard_map/ppermute | solution.py:18
  601.9 105.3 %collective-permute-start.4 = (bf16[2,1200,1024]{2,1,0:T(8,128)(2,1)}, bf16[2,1200,1024]{2,1,0:T(8,128)(2,1)}, u32[]{:S(2)}, u32[]{:S(2)}) collective-permute-start(bf16[2,1200,1024]{2,1,0:T(8,128)(2,1)} %broadcast_select_fusion.3), channel_id=1, source_target_pairs={{0,16},{1,17},{2,18},{3,19},{4,20},{5,21},{6,22},{7,23},{8,24},{9,... | collective-permute-start | bytes 14745608 | tf_op jit(solution)/shard_map/ppermute | solution.py:18
  601.9 108.3 %slice-start = ((s8[4915200]{0:T(1024)(128)(4,1)}), s8[720896]{0:T(1024)(128)(4,1)S(1)}, s32[]{:S(2)}) async-start(s8[4915200]{0:T(1024)(128)(4,1)} %bitcast.41), calls=%async_computation.2 | async-start | bytes 1441792
  601.9 108.3 %slice-start.1 = ((s8[4915200]{0:T(1024)(128)(4,1)}), s8[4194304]{0:T(1024)(128)(4,1)S(1)}, s32[]{:S(2)}) async-start(s8[4915200]{0:T(1024)(128)(4,1)} %bitcast.41), calls=%async_computation.3 | async-start | bytes 8388608
  707.2 6.1 slice-start.2
  710.2 3.1 slice-start.3
  713.3 6.4 copy-start.3
Sparse Core Ops, SparseCore 0:
  719.8 43.6 reduce-scatter.1
where the time goes:
time: 777 us; the launch traced here: 773 us
  waiting for transfers between devices  582 us (75%)
  other arithmetic  89.6 us (12%)
  matrix products  80.6 us (10%)
  between operations  14.5 us (2%)
    ppermute x5, waiting for transfers between devices, shifted(): return lax.ppermute(value, axis, pairs)  541 us
    dot_general x2, matrix products, normalize(): jnp.dot(cosine_table.T, weighted, preferred_element_type=jnp.float32)  71.2 us
    reduce_sum x2, other arithmetic, normalize(): frame_mean = jnp.mean(filtered, axis=0, keepdims=True)  48.3 us
    reduce_scatter x1, waiting for transfers between devices, local(): summed = lax.psum_scatter(running, 'subj', scatter_dimension=0, tiled=True)  41.8 us
    select_n x5, other arithmetic, local(): payload = jnp.where(use_moved, moved, payload)  26.4 us
  transfers between devices with their start and end apart: 6, of which 6 were waited for; matrix products, arithmetic and copies ran while one was open for 0% of the time, Pallas kernels for 0%

commit v1 on v0

v1 whole, which is shorter than its diff:
```python
import functools
import math

import jax
import jax.numpy as jnp
import numpy as np
from jax import lax
from jax.experimental import pallas as pl
from jax.experimental.pallas import tpu as pltpu
from jax.sharding import PartitionSpec as P

tr_seconds = 0.72
low_cut = 0.01
high_cut = 0.08
shrink = 0.98
epsilon = 1e-06
MIB = 1 << 20
TILE = 512


def tables(frames):
    index_row = np.arange(frames, dtype=np.int64)
    product_index = (2 * index_row[None, :] + 1) * index_row[:, None] % (4 * frames)
    phase_angle = product_index.astype(np.float32) * np.float32(math.pi / (2 * frames))
    row_scale = np.where(index_row == 0, math.sqrt(0.5), 1.0).astype(np.float32)
    cosine_table = np.cos(phase_angle.astype(np.float64)).astype(np.float32)
    cosine_table = cosine_table * np.float32(math.sqrt(2.0 / frames)) * row_scale[:, None]
    frequency = index_row.astype(np.float32) / np.float32(2 * frames * tr_seconds)
    high_pass = frequency / low_cut / np.sqrt(1.0 + (frequency / low_cut) ** 2)
    low_pass = 1.0 / np.sqrt(1.0 + (frequency / high_cut) ** 2)
    gains = (high_pass * low_pass).astype(np.float32)[:, None]
    return cosine_table.astype(jnp.bfloat16), gains


def normalize_kernel(series_ref, table_ref, turned_ref, gains_ref, z_ref):
    coefficients = jnp.dot(table_ref[...], series_ref[0], preferred_element_type=jnp.float32)
    weighted = (coefficients * gains_ref[...]).astype(jnp.bfloat16)
    filtered = jnp.dot(turned_ref[...], weighted, preferred_element_type=jnp.float32)
    frame_mean = jnp.mean(filtered, axis=0, keepdims=True)
    centered = filtered - frame_mean
    variance = jnp.mean(centered * centered, axis=0, keepdims=True)
    z_ref[0] = (centered * lax.rsqrt(variance + epsilon)).astype(jnp.bfloat16)


def normalize(series, consts):
    subjects, frames, width = series.shape
    table, turned, gains = consts
    whole = lambda shape: pl.BlockSpec(shape, lambda s, c: (0, 0))
    tile = pl.BlockSpec((1, frames, TILE), lambda s, c: (s, 0, c))
    return pl.pallas_call(
        normalize_kernel,
        grid=(subjects, width // TILE),
        in_specs=[tile, whole(table.shape), whole(turned.shape), whole(gains.shape)],
        out_specs=tile,
        out_shape=jax.ShapeDtypeStruct(series.shape, jnp.bfloat16),
        compiler_params=pltpu.CompilerParams(vmem_limit_bytes=56 * MIB),
        name="normalize",
    )(series, table, turned, gains)


def fisher_kernel(frames, partner_ref, own_ref, sum_ref):
    upper = lower = None
    for subject in range(partner_ref.shape[0]):
        scaled = lax.dot_general(
            partner_ref[subject],
            own_ref[subject],
            (((0,), (0,)), ((), ())),
            preferred_element_type=jnp.float32,
        ) * (shrink / frames)
        upper = 1.0 + scaled if subject == 0 else upper * (1.0 + scaled)
        lower = 1.0 - scaled if subject == 0 else lower * (1.0 - scaled)
    sum_ref[...] = 0.5 * (jnp.log(upper) - jnp.log(lower))


def fisher_sum(partner, own):
    subjects, frames, width = own.shape
    rows = partner.shape[2]
    high = rows // 4
    return pl.pallas_call(
        functools.partial(fisher_kernel, frames),
        grid=(rows // high, width // TILE),
        in_specs=[
            pl.BlockSpec((subjects, frames, high), lambda r, c: (0, 0, r)),
            pl.BlockSpec((subjects, frames, TILE), lambda r, c: (0, 0, c)),
        ],
        out_specs=pl.BlockSpec((high, TILE), lambda r, c: (r, c)),
        out_shape=jax.ShapeDtypeStruct((rows, width), jnp.float32),
        compiler_params=pltpu.CompilerParams(vmem_limit_bytes=56 * MIB),
        name="fisher",
    )(partner, own)


def scatter_sum(part, subj_index):
    rows, width = part.shape
    core = subj_index % 2
    z_half = subj_index // 2
    parts = part.reshape(2, 2, rows // 4, width)
    mine = lax.dynamic_index_in_dim(parts, core, 1, keepdims=False)
    other = lax.dynamic_index_in_dim(parts, 1 - core, 1, keepdims=False)
    near = mine + lax.ppermute(other, "subj", [(d, d ^ 1) for d in range(4)])
    mine = lax.dynamic_index_in_dim(near, z_half, 0, keepdims=False)
    other = lax.dynamic_index_in_dim(near, 1 - z_half, 0, keepdims=False)
    far = lax.ppermute(other.astype(jnp.bfloat16), "subj", [(d, d ^ 2) for d in range(4)])
    return mine + far.astype(jnp.float32)


def local(series, circle_step, vertex_count):
    subj_local, frames, width = series.shape
    table, gains = tables(frames)
    consts = (jnp.asarray(table), jnp.asarray(np.ascontiguousarray(table.T)), jnp.asarray(gains))
    shift_count = circle_step[0]
    block_total = lax.axis_size("blk")
    subj_total = lax.axis_size("subj")
    own_block = lax.axis_index("blk")
    subj_index = lax.axis_index("subj")
    partner = (own_block - shift_count) % block_total
    share = width // subj_total

    own = normalize(series, consts)

    def case(steps):
        pairs = [(source, (source + steps) % block_total) for source in range(block_total)]
        return lambda value: lax.ppermute(value, "blk", pairs)

    arrived = lax.switch(shift_count - 1, [case(steps) for steps in range(1, block_total)], own)
    summed = scatter_sum(fisher_sum(arrived, own), subj_index)

    block_ids = jnp.arange(block_total, dtype=jnp.int32)
    own_count = jnp.sum(jnp.where(block_ids == own_block, vertex_count, 0))
    partner_count = jnp.sum(jnp.where(block_ids == partner, vertex_count, 0))
    row_slots = subj_index * share + jnp.arange(share, dtype=jnp.int32)
    col_slots = jnp.arange(width, dtype=jnp.int32)
    keep_mask = (row_slots < partner_count)[:, None] & (col_slots < own_count)[None, :]
    return jnp.where(keep_mask, summed / (subj_local * subj_total), 0.0)


def solution(mesh):
    in_specs = (P("subj", None, "blk"), P(), P())
    out_specs = P("subj", "blk")
    return jax.shard_map(local, mesh=mesh, in_specs=in_specs, out_specs=out_specs, check_vma=False)
```

time: 777 us -> 175 us (0.23)
  waiting for transfers between devices: 582 us -> 123 us
  other arithmetic: 89.6 us -> 5.87 us
  matrix products: 80.6 us -> 0 us
  Pallas kernels: 0 us -> 35.3 us
  between operations: 14.5 us -> 0.7 us
    ppermute x5 -> x3, waiting for transfers between devices: 541 us -> 123 us  [the longest x1 109 us: case(): return lambda value: lax.ppermute(value, 'blk', pairs)]
    dot_general x4 -> x0, matrix products: 80.6 us -> none  [the longest x2 71.2 us: normalize(): jnp.dot(cosine_table.T, weighted, preferred_element_type=jnp.float32)]
    reduce_sum x4 -> x0, other arithmetic: 54.5 us -> none  [the longest x2 48.3 us: normalize(): frame_mean = jnp.mean(filtered, axis=0, keepdims=True)]
    reduce_scatter x1 -> x0, waiting for transfers between devices: 41.8 us -> none  [local(): summed = lax.psum_scatter(running, 'subj', scatter_dimension=0, tiled=True)]
    pallas_call x0 -> x2, Pallas kernels: none -> 35.3 us  [the longest x1 19.8 us: normalize(): pl.pallas_call(normalize_kernel, grid=(subjects, width // TILE), in_specs...]
    select_n x5 -> x0, other arithmetic: 26.4 us -> none  [local(): payload = jnp.where(use_moved, moved, payload)]
  transfers between devices with their start and end apart: 6 -> 3, of which waited for: 6 -> 3; matrix products, arithmetic and copies ran while one was open for 0% -> 1% of each run, Pallas kernels for 0% -> 0%
where the time goes in v1:
time: 175 us; the launch traced here: 178 us
  waiting for transfers between devices  123 us (70%)
  Pallas kernels  35.3 us (20%)
  starting transfers between devices  8.46 us (5%)
  other arithmetic  5.87 us (3%)
  local copies, waits for them, and re-layouts  4.01 us (2%)
    ppermute x1, waiting for transfers between devices, case(): return lambda value: lax.ppermute(value, 'blk', pairs)  109 us
    pallas_call x1, Pallas kernels, normalize(): pl.pallas_call(normalize_kernel, grid=(subjects, width // TILE), in_specs...  19.8 us
    pallas_call x1, Pallas kernels, fisher_sum(): pl.pallas_call(functools.partial(fisher_kernel, frames), grid=(rows // hi...  15.4 us
    ppermute x1, waiting for transfers between devices, scatter_sum(): lax.ppermute(other.astype(jnp.bfloat16), 'subj', [(d, d ^ 2) for d in ran...  10.3 us
    ppermute x1, starting transfers between devices, case(): return lambda value: lax.ppermute(value, 'blk', pairs)  6.34 us
    ppermute x1, waiting for transfers between devices, scatter_sum(): near = mine + lax.ppermute(other, 'subj', [(d, d ^ 1) for d in range(4)])  3.92 us
  transfers between devices with their start and end apart: 3, of which 3 were waited for; matrix products, arithmetic and copies ran while one was open for 1% of the time, Pallas kernels for 0%

profile of v1, /device:TPU:1, one launch (start us, length us, event | category | flops | bytes accessed | tf_op | source)
XLA Modules:
  0.0 177.6 jit_solution(13878165150919646519)
XLA Ops:
  0.7 19.8 %normalize.1.own_ref = bf16[2,1200,1024]{2,1,0:T(8,128)(2,1)S(1)} custom-call(bf16[2,1200,1024]{2,1,0:T(8,128)(2,1)} %series_ref.1, bf16[1200,1200]{1,0:T(8,128)(2,1)} %constant.76.clone.table_ref, bf16[1200,1200]{1,0:T(8,128)(2,1)} %constant.77.clone.turned_ref, f32[1200,1]{1,0:T(8,128)} %constant.78.clone.gains_ref), custom_call_target="tpu_custom_call" | custom-call | tf_op jit(solution)/shard_map/normalize/pallas_call | solution.py:50
  20.5 0.0 copy-start
  20.5 2.2 %copy-done = bf16[2,1200,1024]{2,1,0:T(8,128)(2,1)} copy-done((bf16[2,1200,1024]{2,1,0:T(8,128)(2,1)}, bf16[2,1200,1024]{2,1,0:T(8,128)(2,1)S(1)}, u32[]{:S(2)}) %copy-start) | copy-done | bytes 4915224
  22.7 115.4 %conditional.1 = (bf16[2,1200,1024]{2,1,0:T(8,128)(2,1)}) conditional(s32[]{:T(128)} %clamp.3, bf16[2,1200,1024]{2,1,0:T(8,128)(2,1)S(1)} %normalize.1.own_ref, bf16[2,1200,1024]{2,1,0:T(8,128)(2,1)S(1)} %normalize.1.own_ref, bf16[2,1200,1024]{2,1,0:T(8,128)(2,1)S(1)} %normalize.1.own_ref, ...), branch_computations={%region_2.3_spmd, %region_3.4_spmd, %region_4.5_spmd, %region_5.6_... | conditional | bytes 19660848 | solution.py:125
  22.7 6.3 %collective-permute-start.10 = (bf16[2,1200,1024]{2,1,0:T(8,128)(2,1)S(1)}, bf16[2,1200,1024]{2,1,0:T(8,128)(2,1)}, u32[]{:S(2)}, u32[]{:S(2)}) collective-permute-start(bf16[2,1200,1024]{2,1,0:T(8,128)(2,1)S(1)} %param.10), channel_id=1, source_target_pairs={{0,11},{1,12},{2,13},{3,14},{4,15},{5,16},{6,17},{7,18},{8,19},{9,... | collective-permute-start | bytes 14745608 | tf_op jit(solution)/shard_map/cond/branch_10_fun/ppermute | solution.py:123
  29.0 109.0 %collective-permute-done.10 = bf16[2,1200,1024]{2,1,0:T(8,128)(2,1)} collective-permute-done((bf16[2,1200,1024]{2,1,0:T(8,128)(2,1)S(1)}, bf16[2,1200,1024]{2,1,0:T(8,128)(2,1)}, u32[]{:S(2)}, u32[]{:S(2)}) %collective-permute-start.10) | collective-permute-done | bytes 4915232 | tf_op jit(solution)/shard_map/cond/branch_10_fun/ppermute | solution.py:123
  138.1 15.4 %fisher.1 = f32[1024,1024]{1,0:T(8,128)} custom-call(bf16[2,1200,1024]{2,1,0:T(8,128)(2,1)} %get-tuple-element.70.partner_ref, bf16[2,1200,1024]{2,1,0:T(8,128)(2,1)} %copy-done), custom_call_target="tpu_custom_call" | custom-call | tf_op jit(solution)/shard_map/fisher/pallas_call | solution.py:79
  153.5 0.0 copy-start.1
  153.5 1.7 dynamic-slice_bitcast_fusion
  155.3 1.3 collective-permute-start.31
  156.6 3.9 %collective-permute-done.31 = f32[2,256,1024]{2,1,0:T(8,128)} collective-permute-done((f32[2,256,1024]{2,1,0:T(8,128)S(1)}, f32[2,256,1024]{2,1,0:T(8,128)}, u32[]{:S(2)}, u32[]{:S(2)}) %collective-permute-start.31) | collective-permute-done | bytes 2097184 | tf_op jit(solution)/shard_map/ppermute | solution.py:100
  160.5 2.6 %bitcast_add_fusion = f32[2,256,1024]{2,1,0:T(8,128)S(1)} fusion(f32[2,256,1024]{2,1,0:T(8,128)} %collective-permute-done.31, f32[2,2,256,1024]{3,2,1,0:T(8,128)} %bitcast.17, s32[]{:T(128)S(6)} %select_n.44), kind=kLoop, calls=%fused_computation | loop fusion | flops 524288 | bytes 6291460 | tf_op jit(solution)/shard_map/add | solution.py:100
  163.1 0.1 fusion.2
  163.2 0.8 collective-permute-start.32
  164.0 0.0 copy-done.1
  164.0 0.7 fusion.3
  164.7 0.7 add_compare_fusion
  165.4 0.7 iota_compare_fusion
  166.1 10.3 %collective-permute-done.32 = bf16[256,1024]{1,0:T(8,128)(2,1)S(1)} collective-permute-done((bf16[256,1024]{1,0:T(8,128)(2,1)S(1)}, bf16[256,1024]{1,0:T(8,128)(2,1)S(1)}, u32[]{:S(2)}, u32[]{:S(2)}) %collective-permute-start.32) | collective-permute-done | bytes 524320 | tf_op jit(solution)/shard_map/ppermute | solution.py:103
  176.4 1.2 fusion.1
Async XLA Ops:
  20.5 2.2 %copy-start = (bf16[2,1200,1024]{2,1,0:T(8,128)(2,1)}, bf16[2,1200,1024]{2,1,0:T(8,128)(2,1)S(1)}, u32[]{:S(2)}) copy-start(bf16[2,1200,1024]{2,1,0:T(8,128)(2,1)S(1)} %normalize.1.own_ref) | copy-start | bytes 14745604
  22.7 115.4 %collective-permute-start.10 = (bf16[2,1200,1024]{2,1,0:T(8,128)(2,1)S(1)}, bf16[2,1200,1024]{2,1,0:T(8,128)(2,1)}, u32[]{:S(2)}, u32[]{:S(2)}) collective-permute-start(bf16[2,1200,1024]{2,1,0:T(8,128)(2,1)S(1)} %param.10), channel_id=1, source_target_pairs={{0,11},{1,12},{2,13},{3,14},{4,15},{5,16},{6,17},{7,18},{8,19},{9,... | collective-permute-start | bytes 14745608 | tf_op jit(solution)/shard_map/cond/branch_10_fun/ppermute | solution.py:123
  153.5 10.5 %copy-start.1 = (s32[32]{0:T(128)S(1)}, s32[32]{0:T(128)}, u32[]{:S(2)}) copy-start(s32[32]{0:T(128)} %param.39) | copy-start | bytes 388
  155.3 5.2 %collective-permute-start.31 = (f32[2,256,1024]{2,1,0:T(8,128)S(1)}, f32[2,256,1024]{2,1,0:T(8,128)}, u32[]{:S(2)}, u32[]{:S(2)}) collective-permute-start(f32[2,256,1024]{2,1,0:T(8,128)S(1)} %dynamic-slice_bitcast_fusion), channel_id=1, source_target_pairs={{0,32},{32,0},{64,96},{96,64},{1,33},{33,1},{65,97},{97,65},{2,34}... | collective-permute-start | bytes 6291464 | tf_op jit(solution)/shard_map/ppermute | solution.py:100
  163.2 13.2 %collective-permute-start.32 = (bf16[256,1024]{1,0:T(8,128)(2,1)S(1)}, bf16[256,1024]{1,0:T(8,128)(2,1)S(1)}, u32[]{:S(2)}, u32[]{:S(2)}) collective-permute-start(bf16[256,1024]{1,0:T(8,128)(2,1)S(1)} %fusion.2), channel_id=1, source_target_pairs={{0,64},{32,96},{64,0},{96,32},{1,65},{33,97},{65,1},{97,33},{2,66}... | collective-permute-start | bytes 1572872 | tf_op jit(solution)/shard_map/ppermute | solution.py:103

commit v2 on v1

v2 whole, which is shorter than its diff:
```python
import functools
import math

import jax
import jax.numpy as jnp
import numpy as np
from jax import lax
from jax.experimental import pallas as pl
from jax.experimental.pallas import tpu as pltpu
from jax.sharding import PartitionSpec as P

tr_seconds = 0.72
low_cut = 0.01
high_cut = 0.08
shrink = 0.98
epsilon = 1e-06
LIMIT = 60 << 20
LANES = 128
TILE = 512
STRIP = 256


def tables(frames):
    index_row = np.arange(frames, dtype=np.int64)
    product_index = (2 * index_row[None, :] + 1) * index_row[:, None] % (4 * frames)
    phase_angle = product_index.astype(np.float32) * np.float32(math.pi / (2 * frames))
    row_scale = np.where(index_row == 0, math.sqrt(0.5), 1.0).astype(np.float32)
    cosine_table = np.cos(phase_angle.astype(np.float64)).astype(np.float32)
    cosine_table = cosine_table * np.float32(math.sqrt(2.0 / frames)) * row_scale[:, None]
    cosine_table = cosine_table.astype(jnp.bfloat16)
    frequency = index_row.astype(np.float32) / np.float32(2 * frames * tr_seconds)
    high_pass = frequency / low_cut / np.sqrt(1.0 + (frequency / low_cut) ** 2)
    low_pass = 1.0 / np.sqrt(1.0 + (frequency / high_cut) ** 2)
    gains = (high_pass * low_pass).astype(np.float32)[:, None]
    half = frames // 2
    analysis = np.zeros((2, half, padded(frames)), cosine_table.dtype)
    synthesis = np.zeros((2, half, padded(half)), cosine_table.dtype)
    for parity in range(2):
        analysis[parity, :, :frames] = cosine_table[parity::2]
        synthesis[parity, :, :half] = cosine_table[parity::2, :half].T
    return analysis, synthesis, np.stack([gains[0::2], gains[1::2]])


def padded(count):
    return -(-count // LANES) * LANES


def normalize_kernel(series_ref, analysis_ref, synthesis_ref, gains_ref, z_ref, raw):
    frames, tile = series_ref.shape[1:]
    half = frames // 2
    raw[:frames] = series_ref[0]
    raw[frames:] = jnp.zeros((raw.shape[0] - frames, tile), raw.dtype)
    parts = []
    for parity in range(2):
        coefficients = jnp.dot(analysis_ref[parity], raw[...], preferred_element_type=jnp.float32)
        weighted = coefficients * gains_ref[parity]
        blank = jnp.zeros((synthesis_ref.shape[2] - half, tile), jnp.float32)
        weighted = jnp.concatenate([weighted, blank], axis=0).astype(jnp.bfloat16)
        parts.append(jnp.dot(synthesis_ref[parity], weighted, preferred_element_type=jnp.float32))
    even, odd = parts
    frame_mean = jnp.sum(even, axis=0, keepdims=True) * (2.0 / frames)
    early = even + odd - frame_mean
    late = even - odd - frame_mean
    squares = jnp.sum(early * early, axis=0, keepdims=True) + jnp.sum(late * late, axis=0, keepdims=True)
    scale = lax.rsqrt(squares / frames + epsilon)
    early, late = early * scale, late * scale
    whole = half // 16 * 16
    z_ref[0, :whole] = early[:whole].astype(jnp.bfloat16)
    z_ref[0, whole : 2 * whole] = late[:whole].astype(jnp.bfloat16)
    rest = jnp.concatenate([early[whole:], late[whole:]], axis=0)
    z_ref[0, 2 * whole :] = rest.astype(jnp.bfloat16)


def normalize(series, consts):
    subjects, frames, width = series.shape
    whole = lambda array: pl.BlockSpec(array.shape, lambda s, c: (0, 0, 0))
    tile = pl.BlockSpec((1, frames, TILE), lambda s, c: (s, 0, c))
    return pl.pallas_call(
        normalize_kernel,
        grid=(subjects, width // TILE),
        in_specs=[tile, *map(whole, consts)],
        out_specs=tile,
        out_shape=jax.ShapeDtypeStruct(series.shape, jnp.bfloat16),
        scratch_shapes=[pltpu.VMEM((padded(frames), TILE), jnp.bfloat16)],
        compiler_params=pltpu.CompilerParams(vmem_limit_bytes=LIMIT),
        name="normalize",
    )(series, *consts)


def fisher_kernel(frames, place_ref, partner_ref, own_ref, near_ref, kept_ref):
    subjects, _, width = own_ref.shape

    def columns(start):
        upper = lower = None
        for subject in range(subjects):
            scaled = lax.dot_general(
                partner_ref[subject],
                own_ref[subject, :, start : start + STRIP],
                (((0,), (0,)), ((), ())),
                preferred_element_type=jnp.float32,
            ) * (shrink / frames)
            upper = 1.0 + scaled if subject == 0 else upper * (1.0 + scaled)
            lower = 1.0 - scaled if subject == 0 else lower * (1.0 - scaled)
        return 0.5 * jnp.log(upper / lower)

    sums = [columns(start) for start in range(0, width, STRIP)]
    for core, sum_ref in enumerate((near_ref, kept_ref)):

        @pl.when(pl.program_id(0) == core)
        def _():
            for strip, value in enumerate(sums):
                sum_ref[:, strip * STRIP : (strip + 1) * STRIP] = value


def fisher_sum(partner, own, z_half, core):
    subjects, frames, width = own.shape
    share = width // 4
    place = jnp.stack([2 * z_half + 1 - core, 2 * z_half + core])
    out = jax.ShapeDtypeStruct((share, width), jnp.float32)
    return pl.pallas_call(
        functools.partial(fisher_kernel, frames),
        grid_spec=pltpu.PrefetchScalarGridSpec(
            num_scalar_prefetch=1,
            grid=(2,),
            in_specs=[
                pl.BlockSpec((subjects, frames, share), lambda r, place: (0, 0, place[r])),
                pl.BlockSpec((subjects, frames, width), lambda r, place: (0, 0, 0)),
            ],
            out_specs=[pl.BlockSpec((share, width), lambda r, place: (0, 0))] * 2,
        ),
        out_shape=[out, out],
        compiler_params=pltpu.CompilerParams(vmem_limit_bytes=LIMIT),
        cost_estimate=pl.CostEstimate(flops=1, bytes_accessed=1, transcendentals=0),
        name="fisher",
    )(place, partner, own)


def local(series, circle_step, vertex_count):
    subj_local, frames, width = series.shape
    consts = tuple(jnp.asarray(value) for value in tables(frames))
    shift_count = circle_step[0]
    block_total = lax.axis_size("blk")
    subj_total = lax.axis_size("subj")
    own_block = lax.axis_index("blk")
    subj_index = lax.axis_index("subj")
    z_half, core = subj_index // 2, subj_index % 2
    partner = (own_block - shift_count) % block_total
    share = width // subj_total

    own = normalize(series, consts)

    def case(steps):
        pairs = [(source, (source + steps) % block_total) for source in range(block_total)]
        return lambda value: lax.ppermute(value, "blk", pairs)

    arrived = lax.switch(shift_count - 1, [case(steps) for steps in range(1, block_total)], own)

    def to_other_core(value):
        return lax.ppermute(value, "subj", [(d, d ^ 1) for d in range(4)])

    near, kept = fisher_sum(arrived, own, 1 - z_half, core)
    leaving = (kept + to_other_core(near)).astype(jnp.bfloat16)
    leaving, z_half = lax.optimization_barrier((leaving, z_half))
    far = lax.ppermute(leaving, "subj", [(d, d ^ 2) for d in range(4)])
    near, kept = fisher_sum(arrived, own, z_half, core)
    near, far = lax.optimization_barrier((near, far))
    summed = kept + to_other_core(near) + far.astype(jnp.float32)

    block_ids = jnp.arange(block_total, dtype=jnp.int32)
    own_count = jnp.sum(jnp.where(block_ids == own_block, vertex_count, 0))
    partner_count = jnp.sum(jnp.where(block_ids == partner, vertex_count, 0))
    row_slots = subj_index * share + jnp.arange(share, dtype=jnp.int32)
    col_slots = jnp.arange(width, dtype=jnp.int32)
    keep_mask = (row_slots < partner_count)[:, None] & (col_slots < own_count)[None, :]
    return jnp.where(keep_mask, summed / (subj_local * subj_total), 0.0)


def solution(mesh):
    in_specs = (P("subj", None, "blk"), P(), P())
    out_specs = P("subj", "blk")
    return jax.shard_map(local, mesh=mesh, in_specs=in_specs, out_specs=out_specs, check_vma=False)
```

time: 175 us -> 164 us (0.937); the launches traced: 178 us -> 165 us
  waiting for transfers between devices: 123 us -> 113 us
  local copies, waits for them, and re-layouts: 4.01 us -> 0.01 us
    ppermute x2 -> x3, waiting for transfers between devices: 14.2 us -> 5.58 us  [the longest x2 3.03 us: to_other_core(): return lax.ppermute(value, 'subj', [(d, d ^ 1) for d in range(4)])]
    add x1 -> x0, other arithmetic: 2.61 us -> none  [scatter_sum(): near = mine + lax.ppermute(other, 'subj', [(d, d ^ 1) for d in range(4)])]
    unnamed x4 -> x2, local copies, waits for them, and re-layouts: 2.19 us -> 0.01 us
    pallas_call x1, Pallas kernels: 19.8 us -> 17.8 us  [normalize(): pl.pallas_call(normalize_kernel, grid=(subjects, width // TILE), in_specs...]
    ppermute x2 -> x3, starting transfers between devices: 2.13 us -> 4.17 us  [the longest x2 2.46 us: to_other_core(): return lax.ppermute(value, 'subj', [(d, d ^ 1) for d in range(4)])]
    pallas_call x1 -> x2, Pallas kernels: 15.4 us -> 17.3 us  [fisher_sum(): pl.pallas_call(functools.partial(fisher_kernel, frames), grid_spec=pltpu....]
    ppermute x1, starting transfers between devices: 6.34 us -> 4.59 us  [case(): return lambda value: lax.ppermute(value, 'blk', pairs)]
  transfers between devices with their start and end apart: 3 -> 4, of which waited for: 3 -> 4; matrix products, arithmetic and copies ran while one was open for 1% -> 2% of each run, Pallas kernels for 0% -> 5%
where the time goes in v2:
time: 164 us; the launch traced here: 165 us
  waiting for transfers between devices  113 us (69%)
  Pallas kernels  35 us (21%)
  starting transfers between devices  8.76 us (5%)
  other arithmetic  6.98 us (4%)
    ppermute x1, waiting for transfers between devices, case(): return lambda value: lax.ppermute(value, 'blk', pairs)  107 us
    pallas_call x1, Pallas kernels, normalize(): pl.pallas_call(normalize_kernel, grid=(subjects, width // TILE), in_specs...  17.8 us
    pallas_call x2, Pallas kernels, fisher_sum(): pl.pallas_call(functools.partial(fisher_kernel, frames), grid_spec=pltpu....  17.3 us
    ppermute x1, starting transfers between devices, case(): return lambda value: lax.ppermute(value, 'blk', pairs)  4.59 us
  transfers between devices with their start and end apart: 4, of which 4 were waited for; matrix products, arithmetic and copies ran while one was open for 2% of the time, Pallas kernels for 5%

profile of v2, /device:TPU:1, one launch (start us, length us, event | category | flops | bytes accessed | tf_op | source)
XLA Modules:
  0.0 164.5 jit_solution(9774645125842885561)
XLA Ops:
  0.7 0.6 pad_add_fusion.place_ref
  1.3 17.8 %normalize.1.own_ref = bf16[2,1200,1024]{2,1,0:T(8,128)(2,1)} custom-call(bf16[2,1200,1024]{2,1,0:T(8,128)(2,1)} %series_ref.1, bf16[2,600,1280]{2,1,0:T(8,128)(2,1)} %constant.61.clone.analysis_ref, bf16[2,600,640]{2,1,0:T(8,128)(2,1)} %constant.62.clone.synthesis_ref, f32[2,600,1]{2,1,0:T(8,128)} %constant.63.clone.gains_ref), custom_call_target="tpu_custom_call" | custom-call | tf_op jit(solution)/shard_map/normalize/pallas_call | solution.py:78
  19.1 112.0 %conditional.1 = (bf16[2,1200,1024]{2,1,0:T(8,128)(2,1)}) conditional(s32[]{:T(128)} %clamp.3, bf16[2,1200,1024]{2,1,0:T(8,128)(2,1)} %normalize.1.own_ref, bf16[2,1200,1024]{2,1,0:T(8,128)(2,1)} %normalize.1.own_ref, bf16[2,1200,1024]{2,1,0:T(8,128)(2,1)} %normalize.1.own_ref, ...), branch_computations={%region_2.3_spmd, %region_3.4_spmd, %region_4.5_spmd, %region_5.6_... | conditional | bytes 19660848 | solution.py:156
  19.1 4.6 %collective-permute-start.11 = (bf16[2,1200,1024]{2,1,0:T(8,128)(2,1)}, bf16[2,1200,1024]{2,1,0:T(8,128)(2,1)}, u32[]{:S(2)}, u32[]{:S(2)}) collective-permute-start(bf16[2,1200,1024]{2,1,0:T(8,128)(2,1)} %param.11), channel_id=1, source_target_pairs={{0,12},{1,13},{2,14},{3,15},{4,16},{5,17},{6,18},{7,19},{8,20},{9,... | collective-permute-start | bytes 14745608 | tf_op jit(solution)/shard_map/cond/branch_11_fun/ppermute | solution.py:154
  23.6 107.5 %collective-permute-done.11 = bf16[2,1200,1024]{2,1,0:T(8,128)(2,1)} collective-permute-done((bf16[2,1200,1024]{2,1,0:T(8,128)(2,1)}, bf16[2,1200,1024]{2,1,0:T(8,128)(2,1)}, u32[]{:S(2)}, u32[]{:S(2)}) %collective-permute-start.11) | collective-permute-done | bytes 4915232 | tf_op jit(solution)/shard_map/cond/branch_11_fun/ppermute | solution.py:154
  131.1 8.6 %fisher.2 = (f32[256,1024]{1,0:T(8,128)}, f32[256,1024]{1,0:T(8,128)}) custom-call(s32[2]{0:T(128)} %pad_add_fusion.place_ref, bf16[2,1200,1024]{2,1,0:T(8,128)(2,1)} %get-tuple-element.86.partner_ref, bf16[2,1200,1024]{2,1,0:T(8,128)(2,1)} %normalize.1.own_ref), custom_call_target="tpu_custom_call" | custom-call | flops 1 | bytes 1 | tf_op jit(solution)/shard_map/fisher/pallas_call | solution.py:120
  139.7 1.4 collective-permute-start.31
  141.1 2.5 %collective-permute-done.31 = f32[256,1024]{1,0:T(8,128)S(1)} collective-permute-done((f32[256,1024]{1,0:T(8,128)}, f32[256,1024]{1,0:T(8,128)S(1)}, u32[]{:S(2)}, u32[]{:S(2)}) %collective-permute-start.31) | collective-permute-done | bytes 1048608 | tf_op jit(solution)/shard_map/ppermute | solution.py:159
  143.6 1.4 add_convert_fusion
  145.0 1.7 %collective-permute-start.32 = (bf16[256,1024]{1,0:T(8,128)(2,1)S(1)}, bf16[256,1024]{1,0:T(8,128)(2,1)S(1)}, u32[]{:S(2)}, u32[]{:S(2)}) collective-permute-start(bf16[256,1024]{1,0:T(8,128)(2,1)S(1)} %add_convert_fusion), channel_id=1, source_target_pairs={{0,64},{32,96},{64,0},{96,32},{1,65},{33,97},{65,1},{97,33},{2,66}... | collective-permute-start | bytes 1572872 | tf_op jit(solution)/shard_map/ppermute | solution.py:164
  146.7 0.6 pad_add_fusion.1.place_ref
  147.3 0.0 copy-start
  147.3 8.7 %fisher.3 = (f32[256,1024]{1,0:T(8,128)}, f32[256,1024]{1,0:T(8,128)}) custom-call(s32[2]{0:T(128)} %pad_add_fusion.1.place_ref, bf16[2,1200,1024]{2,1,0:T(8,128)(2,1)} %get-tuple-element.86.partner_ref, bf16[2,1200,1024]{2,1,0:T(8,128)(2,1)} %normalize.1.own_ref), custom_call_target="tpu_custom_call" | custom-call | flops 1 | bytes 1 | tf_op jit(solution)/shard_map/fisher/pallas_call | solution.py:120
  156.0 2.6 %collective-permute-done.32 = bf16[256,1024]{1,0:T(8,128)(2,1)S(1)} collective-permute-done((bf16[256,1024]{1,0:T(8,128)(2,1)S(1)}, bf16[256,1024]{1,0:T(8,128)(2,1)S(1)}, u32[]{:S(2)}, u32[]{:S(2)}) %collective-permute-start.32) | collective-permute-done | bytes 524320 | tf_op jit(solution)/shard_map/ppermute | solution.py:164
  158.5 1.0 collective-permute-start.33
  159.6 0.0 copy-done
  159.6 0.7 fusion
  160.3 0.6 add_compare_fusion
  160.9 0.6 iota_compare_fusion
  161.5 0.5 collective-permute-done.33
  162.1 2.4 %multiply_select_fusion = f32[256,1024]{1,0:T(8,128)} fusion(bf16[256,1024]{1,0:T(8,128)(2,1)S(1)} %collective-permute-done.32, f32[256,1024]{1,0:T(8,128)} %get-tuple-element.79, f32[256,1024]{1,0:T(8,128)S(1)} %collective-permute-done.33, pred[1024]{0:T(1024)(128)(4,1)S(1)} %iota_compare_fusion, pred[256]{0:T(512)(128)(4,1)S(1)} %add_compare_fusion), kind=kLoop, calls=%fused_computation | loop fusion | flops 1572864 | bytes 3671296 | tf_op jit(solution)/shard_map/jit(_where)/select_n | solution.py:175
Async XLA Ops:
  19.1 112.0 %collective-permute-start.11 = (bf16[2,1200,1024]{2,1,0:T(8,128)(2,1)}, bf16[2,1200,1024]{2,1,0:T(8,128)(2,1)}, u32[]{:S(2)}, u32[]{:S(2)}) collective-permute-start(bf16[2,1200,1024]{2,1,0:T(8,128)(2,1)} %param.11), channel_id=1, source_target_pairs={{0,12},{1,13},{2,14},{3,15},{4,16},{5,17},{6,18},{7,19},{8,20},{9,... | collective-permute-start | bytes 14745608 | tf_op jit(solution)/shard_map/cond/branch_11_fun/ppermute | solution.py:154
  139.7 3.9 %collective-permute-start.31 = (f32[256,1024]{1,0:T(8,128)}, f32[256,1024]{1,0:T(8,128)S(1)}, u32[]{:S(2)}, u32[]{:S(2)}) collective-permute-start(f32[256,1024]{1,0:T(8,128)} %get-tuple-element.77), channel_id=1, source_target_pairs={{0,32},{32,0},{64,96},{96,64},{1,33},{33,1},{65,97},{97,65},{2,34}... | collective-permute-start | bytes 3145736 | tf_op jit(solution)/shard_map/ppermute | solution.py:159
  145.0 13.6 %collective-permute-start.32 = (bf16[256,1024]{1,0:T(8,128)(2,1)S(1)}, bf16[256,1024]{1,0:T(8,128)(2,1)S(1)}, u32[]{:S(2)}, u32[]{:S(2)}) collective-permute-start(bf16[256,1024]{1,0:T(8,128)(2,1)S(1)} %add_convert_fusion), channel_id=1, source_target_pairs={{0,64},{32,96},{64,0},{96,32},{1,65},{33,97},{65,1},{97,33},{2,66}... | collective-permute-start | bytes 1572872 | tf_op jit(solution)/shard_map/ppermute | solution.py:164
  147.3 12.3 %copy-start = (s32[32]{0:T(128)S(1)}, s32[32]{0:T(128)}, u32[]{:S(2)}) copy-start(s32[32]{0:T(128)} %param.39) | copy-start | bytes 388
  158.5 3.5 %collective-permute-start.33 = (f32[256,1024]{1,0:T(8,128)}, f32[256,1024]{1,0:T(8,128)S(1)}, u32[]{:S(2)}, u32[]{:S(2)}) collective-permute-start(f32[256,1024]{1,0:T(8,128)} %get-tuple-element.82), channel_id=1, source_target_pairs={{0,32},{32,0},{64,96},{96,64},{1,33},{33,1},{65,97},{97,65},{2,34}... | collective-permute-start | bytes 3145736 | tf_op jit(solution)/shard_map/ppermute | solution.py:159

commit v3 on v2

--- a/solution.py
+++ b/solution.py
@@ -15,6 +15,7 @@
 shrink = 0.98
 epsilon = 1e-06
 LIMIT = 60 << 20
+FISHER_LIMIT = 40 << 20
 LANES = 128
 TILE = 512
 STRIP = 256
@@ -112,10 +113,9 @@
                 sum_ref[:, strip * STRIP : (strip + 1) * STRIP] = value
 
 
-def fisher_sum(partner, own, z_half, core):
+def fisher_sum(partner, own, place):
     subjects, frames, width = own.shape
     share = width // 4
-    place = jnp.stack([2 * z_half + 1 - core, 2 * z_half + core])
     out = jax.ShapeDtypeStruct((share, width), jnp.float32)
     return pl.pallas_call(
         functools.partial(fisher_kernel, frames),
@@ -129,7 +129,7 @@
             out_specs=[pl.BlockSpec((share, width), lambda r, place: (0, 0))] * 2,
         ),
         out_shape=[out, out],
-        compiler_params=pltpu.CompilerParams(vmem_limit_bytes=LIMIT),
+        compiler_params=pltpu.CompilerParams(vmem_limit_bytes=FISHER_LIMIT),
         cost_estimate=pl.CostEstimate(flops=1, bytes_accessed=1, transcendentals=0),
         name="fisher",
     )(place, partner, own)
@@ -143,7 +143,8 @@
     subj_total = lax.axis_size("subj")
     own_block = lax.axis_index("blk")
     subj_index = lax.axis_index("subj")
-    z_half, core = subj_index // 2, subj_index % 2
+    places = subj_index ^ jnp.array([3, 2, 1, 0], jnp.int32)
+    other_chip, this_chip = places[:2], places[2:]
     partner = (own_block - shift_count) % block_total
     share = width // subj_total
 
@@ -158,11 +159,11 @@
     def to_other_core(value):
         return lax.ppermute(value, "subj", [(d, d ^ 1) for d in range(4)])
 
-    near, kept = fisher_sum(arrived, own, 1 - z_half, core)
+    near, kept = fisher_sum(arrived, own, other_chip)
     leaving = (kept + to_other_core(near)).astype(jnp.bfloat16)
-    leaving, z_half = lax.optimization_barrier((leaving, z_half))
+    leaving, this_chip = lax.optimization_barrier((leaving, this_chip))
     far = lax.ppermute(leaving, "subj", [(d, d ^ 2) for d in range(4)])
-    near, kept = fisher_sum(arrived, own, z_half, core)
+    near, kept = fisher_sum(arrived, own, this_chip)
     near, far = lax.optimization_barrier((near, far))
     summed = kept + to_other_core(near) + far.astype(jnp.float32)
 

time: 164 us -> 163 us (level)
  Pallas kernels: 35 us -> 31 us
  waiting for transfers between devices: 113 us -> 115 us
  other arithmetic: 6.98 us -> 5.11 us
  starting transfers between devices: 8.76 us -> 10.4 us
    pallas_call x2, Pallas kernels: 17.3 us -> 13.2 us  [fisher_sum(): pl.pallas_call(functools.partial(fisher_kernel, frames), grid_spec=pltpu....]
    ppermute x1, waiting for transfers between devices: 2.55 us -> 6.41 us  [local(): far = lax.ppermute(leaving, 'subj', [(d, d ^ 2) for d in range(4)])]
    ppermute x1, starting transfers between devices: 4.59 us -> 6.88 us  [case(): return lambda value: lax.ppermute(value, 'blk', pairs)]
    ppermute x1, waiting for transfers between devices: 107 us -> 106 us  [case(): return lambda value: lax.ppermute(value, 'blk', pairs)]
  transfers between devices with their start and end apart: 4 -> 4, of which waited for: 4 -> 4; matrix products, arithmetic and copies ran while one was open for 2% -> 1% of each run, Pallas kernels for 5% -> 4%
where the time goes in v3:
time: 163 us
  waiting for transfers between devices  115 us (71%)
  Pallas kernels  31 us (19%)
  starting transfers between devices  10.4 us (6%)
  other arithmetic  5.11 us (3%)
    ppermute x1, waiting for transfers between devices, case(): return lambda value: lax.ppermute(value, 'blk', pairs)  106 us
    pallas_call x1, Pallas kernels, normalize(): pl.pallas_call(normalize_kernel, grid=(subjects, width // TILE), in_specs...  17.8 us
    pallas_call x2, Pallas kernels, fisher_sum(): pl.pallas_call(functools.partial(fisher_kernel, frames), grid_spec=pltpu....  13.2 us
    ppermute x1, starting transfers between devices, case(): return lambda value: lax.ppermute(value, 'blk', pairs)  6.88 us
    ppermute x1, waiting for transfers between devices, local(): far = lax.ppermute(leaving, 'subj', [(d, d ^ 2) for d in range(4)])  6.41 us
  transfers between devices with their start and end apart: 4, of which 4 were waited for; matrix products, arithmetic and copies ran while one was open for 1% of the time, Pallas kernels for 4%

profile of v3, /device:TPU:1, one launch (start us, length us, event | category | flops | bytes accessed | tf_op | source)
XLA Modules:
  0.0 162.9 jit_solution(6047903762415104320)
XLA Ops:
  0.7 0.7 broadcast_xor_fusion
  1.3 0.1 fusion.2
  1.4 17.8 %normalize.1.own_ref = bf16[2,1200,1024]{2,1,0:T(8,128)(2,1)} custom-call(bf16[2,1200,1024]{2,1,0:T(8,128)(2,1)} %series_ref.1, bf16[2,600,1280]{2,1,0:T(8,128)(2,1)} %constant.43.clone.analysis_ref, bf16[2,600,640]{2,1,0:T(8,128)(2,1)} %constant.44.clone.synthesis_ref, f32[2,600,1]{2,1,0:T(8,128)} %constant.45.clone.gains_ref), custom_call_target="tpu_custom_call" | custom-call | tf_op jit(solution)/shard_map/normalize/pallas_call | solution.py:79
  19.2 112.7 %conditional.1 = (bf16[2,1200,1024]{2,1,0:T(8,128)(2,1)}) conditional(s32[]{:T(128)} %clamp.3, bf16[2,1200,1024]{2,1,0:T(8,128)(2,1)} %normalize.1.own_ref, bf16[2,1200,1024]{2,1,0:T(8,128)(2,1)} %normalize.1.own_ref, bf16[2,1200,1024]{2,1,0:T(8,128)(2,1)} %normalize.1.own_ref, ...), branch_computations={%region_2.3_spmd, %region_3.4_spmd, %region_4.5_spmd, %region_5.6_... | conditional | bytes 19660848 | solution.py:157
  19.2 6.9 %collective-permute-start.24 = (bf16[2,1200,1024]{2,1,0:T(8,128)(2,1)}, bf16[2,1200,1024]{2,1,0:T(8,128)(2,1)}, u32[]{:S(2)}, u32[]{:S(2)}) collective-permute-start(bf16[2,1200,1024]{2,1,0:T(8,128)(2,1)} %param.24), channel_id=1, source_target_pairs={{0,25},{1,26},{2,27},{3,28},{4,29},{5,30},{6,31},{7,0},{8,1},{9,2}... | collective-permute-start | bytes 14745608 | tf_op jit(solution)/shard_map/cond/branch_24_fun/ppermute | solution.py:155
  26.1 105.8 %collective-permute-done.24 = bf16[2,1200,1024]{2,1,0:T(8,128)(2,1)} collective-permute-done((bf16[2,1200,1024]{2,1,0:T(8,128)(2,1)}, bf16[2,1200,1024]{2,1,0:T(8,128)(2,1)}, u32[]{:S(2)}, u32[]{:S(2)}) %collective-permute-start.24) | collective-permute-done | bytes 4915232 | tf_op jit(solution)/shard_map/cond/branch_24_fun/ppermute | solution.py:155
  131.9 0.0 slice-start
  131.9 0.0 slice-start.1
  131.9 7.4 %fisher.2 = (f32[256,1024]{1,0:T(8,128)S(1)}, f32[256,1024]{1,0:T(8,128)S(1)}) custom-call(s32[2]{0:T(128)S(1)} %get-tuple-element.87.place_ref, bf16[2,1200,1024]{2,1,0:T(8,128)(2,1)} %get-tuple-element.88.partner_ref, bf16[2,1200,1024]{2,1,0:T(8,128)(2,1)} %normalize.1.own_ref), custom_call_target="tpu_custom_call" | custom-call | flops 1 | bytes 1 | tf_op jit(solution)/shard_map/fisher/pallas_call | solution.py:120
  139.3 1.3 collective-permute-start.31
  140.6 2.3 %collective-permute-done.31 = f32[256,1024]{1,0:T(8,128)S(1)} collective-permute-done((f32[256,1024]{1,0:T(8,128)S(1)}, f32[256,1024]{1,0:T(8,128)S(1)}, u32[]{:S(2)}, u32[]{:S(2)}) %collective-permute-start.31) | collective-permute-done | bytes 1048608 | tf_op jit(solution)/shard_map/ppermute | solution.py:160
  142.9 0.2 add_convert_fusion
  143.1 0.0 copy-start.1
  143.1 1.0 collective-permute-start.32
  144.1 0.0 slice-done
  144.1 0.0 slice-done.1
  144.1 5.8 %fisher.3 = (f32[256,1024]{1,0:T(8,128)S(1)}, f32[256,1024]{1,0:T(8,128)S(1)}) custom-call(s32[2]{0:T(128)S(1)} %get-tuple-element.78.place_ref, bf16[2,1200,1024]{2,1,0:T(8,128)(2,1)} %get-tuple-element.88.partner_ref, bf16[2,1200,1024]{2,1,0:T(8,128)(2,1)S(1)} %bitcast.4), custom_call_target="tpu_custom_call" | custom-call | flops 1 | bytes 1 | tf_op jit(solution)/shard_map/fisher/pallas_call | solution.py:120
  149.9 6.4 %collective-permute-done.32 = bf16[256,1024]{1,0:T(8,128)(2,1)S(1)} collective-permute-done((bf16[256,1024]{1,0:T(8,128)(2,1)S(1)}, bf16[256,1024]{1,0:T(8,128)(2,1)S(1)}, u32[]{:S(2)}, u32[]{:S(2)}) %collective-permute-start.32) | collective-permute-done | bytes 524320 | tf_op jit(solution)/shard_map/ppermute | solution.py:165
  156.3 0.0 copy-start
  156.3 0.8 copy-done
  157.1 1.2 collective-permute-start.33
  158.3 0.0 copy-done.1
  158.3 0.7 fusion
  159.0 0.7 add_compare_fusion
  159.7 0.6 iota_compare_fusion
  160.3 0.3 collective-permute-done.33
  160.6 2.3 %multiply_select_fusion = f32[256,1024]{1,0:T(8,128)} fusion(bf16[256,1024]{1,0:T(8,128)(2,1)} %copy-done, f32[256,1024]{1,0:T(8,128)S(1)} %get-tuple-element.79, f32[256,1024]{1,0:T(8,128)S(1)} %collective-permute-done.33, pred[1024]{0:T(1024)(128)(4,1)S(1)} %iota_compare_fusion, pred[256]{0:T(512)(128)(4,1)S(1)} %add_compare_fusion), kind=kLoop, calls=%fused_computation | loop fusion | flops 1572864 | bytes 3671296 | tf_op jit(solution)/shard_map/jit(_where)/select_n | solution.py:176
  (1 shorter events, 0.0 us)
Async XLA Ops:
  19.2 112.7 %collective-permute-start.24 = (bf16[2,1200,1024]{2,1,0:T(8,128)(2,1)}, bf16[2,1200,1024]{2,1,0:T(8,128)(2,1)}, u32[]{:S(2)}, u32[]{:S(2)}) collective-permute-start(bf16[2,1200,1024]{2,1,0:T(8,128)(2,1)} %param.24), channel_id=1, source_target_pairs={{0,25},{1,26},{2,27},{3,28},{4,29},{5,30},{6,31},{7,0},{8,1},{9,2}... | collective-permute-start | bytes 14745608 | tf_op jit(solution)/shard_map/cond/branch_24_fun/ppermute | solution.py:155
  131.9 12.2 %slice-start = ((s8[4915200]{0:T(1024)(128)(4,1)}), s8[4194304]{0:T(1024)(128)(4,1)S(1)}, s32[]{:S(2)}) async-start(s8[4915200]{0:T(1024)(128)(4,1)} %bitcast.3), calls=%async_computation | async-start | bytes 8388608
  131.9 12.2 %slice-start.1 = ((s8[4915200]{0:T(1024)(128)(4,1)}), s8[720896]{0:T(1024)(128)(4,1)S(1)}, s32[]{:S(2)}) async-start(s8[4915200]{0:T(1024)(128)(4,1)} %bitcast.3), calls=%async_computation.1 | async-start | bytes 1441792
  139.3 3.6 %collective-permute-start.31 = (f32[256,1024]{1,0:T(8,128)S(1)}, f32[256,1024]{1,0:T(8,128)S(1)}, u32[]{:S(2)}, u32[]{:S(2)}) collective-permute-start(f32[256,1024]{1,0:T(8,128)S(1)} %get-tuple-element.77), channel_id=1, source_target_pairs={{0,32},{32,0},{64,96},{96,64},{1,33},{33,1},{65,97},{97,65},{2,34}... | collective-permute-start | bytes 3145736 | tf_op jit(solution)/shard_map/ppermute | solution.py:160
  143.1 15.2 %copy-start.1 = (s32[32]{0:T(128)S(1)}, s32[32]{0:T(128)}, u32[]{:S(2)}) copy-start(s32[32]{0:T(128)} %param.40) | copy-start | bytes 388
  143.1 13.2 %collective-permute-start.32 = (bf16[256,1024]{1,0:T(8,128)(2,1)S(1)}, bf16[256,1024]{1,0:T(8,128)(2,1)S(1)}, u32[]{:S(2)}, u32[]{:S(2)}) collective-permute-start(bf16[256,1024]{1,0:T(8,128)(2,1)S(1)} %add_convert_fusion), channel_id=1, source_target_pairs={{0,64},{32,96},{64,0},{96,32},{1,65},{33,97},{65,1},{97,33},{2,66}... | collective-permute-start | bytes 1572872 | tf_op jit(solution)/shard_map/ppermute | solution.py:165
  156.3 0.8 copy-start
  157.1 3.5 %collective-permute-start.33 = (f32[256,1024]{1,0:T(8,128)S(1)}, f32[256,1024]{1,0:T(8,128)S(1)}, u32[]{:S(2)}, u32[]{:S(2)}) collective-permute-start(f32[256,1024]{1,0:T(8,128)S(1)} %get-tuple-element.82), channel_id=1, source_target_pairs={{0,32},{32,0},{64,96},{96,64},{1,33},{33,1},{65,97},{97,65},{2,34}... | collective-permute-start | bytes 3145736 | tf_op jit(solution)/shard_map/ppermute | solution.py:160

commit v4 on v3

--- a/solution.py
+++ b/solution.py
@@ -113,7 +113,7 @@
                 sum_ref[:, strip * STRIP : (strip + 1) * STRIP] = value
 
 
-def fisher_sum(partner, own, place):
+def fisher_sum(partner, own, place, chip):
     subjects, frames, width = own.shape
     share = width // 4
     out = jax.ShapeDtypeStruct((share, width), jnp.float32)
@@ -123,7 +123,7 @@
             num_scalar_prefetch=1,
             grid=(2,),
             in_specs=[
-                pl.BlockSpec((subjects, frames, share), lambda r, place: (0, 0, place[r])),
+                pl.BlockSpec((subjects, frames, share), lambda r, place: (0, 0, place[0] ^ (2 * chip + 1 - r))),
                 pl.BlockSpec((subjects, frames, width), lambda r, place: (0, 0, 0)),
             ],
             out_specs=[pl.BlockSpec((share, width), lambda r, place: (0, 0))] * 2,
@@ -132,7 +132,7 @@
         compiler_params=pltpu.CompilerParams(vmem_limit_bytes=FISHER_LIMIT),
         cost_estimate=pl.CostEstimate(flops=1, bytes_accessed=1, transcendentals=0),
         name="fisher",
-    )(place, partner, own)
+    )(place[None], partner, own)
 
 
 def local(series, circle_step, vertex_count):
@@ -143,8 +143,6 @@
     subj_total = lax.axis_size("subj")
     own_block = lax.axis_index("blk")
     subj_index = lax.axis_index("subj")
-    places = subj_index ^ jnp.array([3, 2, 1, 0], jnp.int32)
-    other_chip, this_chip = places[:2], places[2:]
     partner = (own_block - shift_count) % block_total
     share = width // subj_total
 
@@ -159,13 +157,15 @@
     def to_other_core(value):
         return lax.ppermute(value, "subj", [(d, d ^ 1) for d in range(4)])
 
-    near, kept = fisher_sum(arrived, own, other_chip)
+    near, kept = fisher_sum(arrived, own, subj_index, 1)
     leaving = (kept + to_other_core(near)).astype(jnp.bfloat16)
-    leaving, this_chip = lax.optimization_barrier((leaving, this_chip))
+    leaving, place = lax.optimization_barrier((leaving, subj_index))
     far = lax.ppermute(leaving, "subj", [(d, d ^ 2) for d in range(4)])
-    near, kept = fisher_sum(arrived, own, this_chip)
+    near, kept = fisher_sum(arrived, own, place, 0)
     near, far = lax.optimization_barrier((near, far))
-    summed = kept + to_other_core(near) + far.astype(jnp.float32)
+    near = to_other_core(near)
+    kept, near = lax.optimization_barrier((kept + far.astype(jnp.float32), near))
+    summed = kept + near
 
     block_ids = jnp.arange(block_total, dtype=jnp.int32)
     own_count = jnp.sum(jnp.where(block_ids == own_block, vertex_count, 0))

time: 163 us -> 163 us (level)
  transfers between devices with their start and end apart: 4 -> 4, of which waited for: 4 -> 3; matrix products, arithmetic and copies ran while one was open for 1% -> 2% of each run, Pallas kernels for 4% -> 3%
where the time goes in v4:
time: 163 us; the launch traced here: 162 us
  waiting for transfers between devices  115 us (71%)
  Pallas kernels  29.7 us (18%)
  starting transfers between devices  11.4 us (7%)
  other arithmetic  4.42 us (3%)
    ppermute x1, waiting for transfers between devices, case(): return lambda value: lax.ppermute(value, 'blk', pairs)  106 us
    pallas_call x1, Pallas kernels, normalize(): pl.pallas_call(normalize_kernel, grid=(subjects, width // TILE), in_specs...  17.8 us
    pallas_call x2, Pallas kernels, fisher_sum(): pl.pallas_call(functools.partial(fisher_kernel, frames), grid_spec=pltpu....  11.8 us
    ppermute x1, starting transfers between devices, case(): return lambda value: lax.ppermute(value, 'blk', pairs)  7.99 us
    ppermute x1, waiting for transfers between devices, local(): far = lax.ppermute(leaving, 'subj', [(d, d ^ 2) for d in range(4)])  7.18 us
  transfers between devices with their start and end apart: 4, of which 3 were waited for; matrix products, arithmetic and copies ran while one was open for 2% of the time, Pallas kernels for 3%

profile of v4, /device:TPU:1, one launch (start us, length us, event | category | flops | bytes accessed | tf_op | source)
XLA Modules:
  0.0 162.5 jit_solution(3357528580186613601)
XLA Ops:
  0.7 17.8 %normalize.1.own_ref = bf16[2,1200,1024]{2,1,0:T(8,128)(2,1)} custom-call(bf16[2,1200,1024]{2,1,0:T(8,128)(2,1)} %series_ref.1, bf16[2,600,1280]{2,1,0:T(8,128)(2,1)} %constant.41.clone.analysis_ref, bf16[2,600,640]{2,1,0:T(8,128)(2,1)} %constant.42.clone.synthesis_ref, f32[2,600,1]{2,1,0:T(8,128)} %constant.43.clone.gains_ref), custom_call_target="tpu_custom_call" | custom-call | tf_op jit(solution)/shard_map/normalize/pallas_call | solution.py:79
  18.5 114.0 %conditional.1 = (bf16[2,1200,1024]{2,1,0:T(8,128)(2,1)}) conditional(s32[]{:T(128)} %clamp.3, bf16[2,1200,1024]{2,1,0:T(8,128)(2,1)} %normalize.1.own_ref, bf16[2,1200,1024]{2,1,0:T(8,128)(2,1)} %normalize.1.own_ref, bf16[2,1200,1024]{2,1,0:T(8,128)(2,1)} %normalize.1.own_ref, ...), branch_computations={%region_2.3_spmd, %region_3.4_spmd, %region_4.5_spmd, %region_5.6_... | conditional | bytes 19660848 | solution.py:155
  18.5 8.0 %collective-permute-start.18 = (bf16[2,1200,1024]{2,1,0:T(8,128)(2,1)}, bf16[2,1200,1024]{2,1,0:T(8,128)(2,1)}, u32[]{:S(2)}, u32[]{:S(2)}) collective-permute-start(bf16[2,1200,1024]{2,1,0:T(8,128)(2,1)} %param.18), channel_id=1, source_target_pairs={{0,19},{1,20},{2,21},{3,22},{4,23},{5,24},{6,25},{7,26},{8,27},{9,... | collective-permute-start | bytes 14745608 | tf_op jit(solution)/shard_map/cond/branch_18_fun/ppermute | solution.py:153
  26.5 106.0 %collective-permute-done.18 = bf16[2,1200,1024]{2,1,0:T(8,128)(2,1)} collective-permute-done((bf16[2,1200,1024]{2,1,0:T(8,128)(2,1)}, bf16[2,1200,1024]{2,1,0:T(8,128)(2,1)}, u32[]{:S(2)}, u32[]{:S(2)}) %collective-permute-start.18) | collective-permute-done | bytes 4915232 | tf_op jit(solution)/shard_map/cond/branch_18_fun/ppermute | solution.py:153
  132.5 0.0 slice-start
  132.5 0.0 slice-start.1
  132.5 6.7 %fisher.2 = (f32[256,1024]{1,0:T(8,128)S(1)}, f32[256,1024]{1,0:T(8,128)S(1)}) custom-call(s32[1]{0:T(128)} %bitcast.1.place_ref, bf16[2,1200,1024]{2,1,0:T(8,128)(2,1)} %get-tuple-element.90.partner_ref, bf16[2,1200,1024]{2,1,0:T(8,128)(2,1)} %normalize.1.own_ref), custom_call_target="tpu_custom_call" | custom-call | flops 1 | bytes 1 | tf_op jit(solution)/shard_map/fisher/pallas_call | solution.py:120
  139.2 1.3 collective-permute-start.31
  140.5 2.3 %collective-permute-done.31 = f32[256,1024]{1,0:T(8,128)S(1)} collective-permute-done((f32[256,1024]{1,0:T(8,128)S(1)}, f32[256,1024]{1,0:T(8,128)S(1)}, u32[]{:S(2)}, u32[]{:S(2)}) %collective-permute-start.31) | collective-permute-done | bytes 1048608 | tf_op jit(solution)/shard_map/ppermute | solution.py:158
  142.8 0.2 add_convert_fusion
  143.0 0.9 collective-permute-start.32
  143.9 0.0 slice-done
  143.9 0.0 slice-done.1
  143.9 0.0 copy-start.1
  143.9 5.1 %fisher.3 = (f32[256,1024]{1,0:T(8,128)S(1)}, f32[256,1024]{1,0:T(8,128)S(1)}) custom-call(s32[1]{0:T(128)} %bitcast.2.place_ref, bf16[2,1200,1024]{2,1,0:T(8,128)(2,1)} %get-tuple-element.90.partner_ref, bf16[2,1200,1024]{2,1,0:T(8,128)(2,1)S(1)} %bitcast.6), custom_call_target="tpu_custom_call" | custom-call | flops 1 | bytes 1 | tf_op jit(solution)/shard_map/fisher/pallas_call | solution.py:120
  149.0 7.2 %collective-permute-done.32 = bf16[256,1024]{1,0:T(8,128)(2,1)S(1)} collective-permute-done((bf16[256,1024]{1,0:T(8,128)(2,1)S(1)}, bf16[256,1024]{1,0:T(8,128)(2,1)S(1)}, u32[]{:S(2)}, u32[]{:S(2)}) %collective-permute-start.32) | collective-permute-done | bytes 524320 | tf_op jit(solution)/shard_map/ppermute | solution.py:163
  156.2 0.0 copy-start
  156.2 0.8 copy-done
  157.0 1.2 collective-permute-start.33
  158.2 0.0 copy-done.1
  158.2 0.6 fusion
  158.8 0.6 add_compare_fusion
  159.4 0.6 iota_compare_fusion
  160.0 1.2 convert_add_fusion
  161.2 0.0 collective-permute-done.33
  161.2 1.2 multiply_select_fusion
  (1 shorter events, 0.0 us)
Async XLA Ops:
  18.5 114.0 %collective-permute-start.18 = (bf16[2,1200,1024]{2,1,0:T(8,128)(2,1)}, bf16[2,1200,1024]{2,1,0:T(8,128)(2,1)}, u32[]{:S(2)}, u32[]{:S(2)}) collective-permute-start(bf16[2,1200,1024]{2,1,0:T(8,128)(2,1)} %param.18), channel_id=1, source_target_pairs={{0,19},{1,20},{2,21},{3,22},{4,23},{5,24},{6,25},{7,26},{8,27},{9,... | collective-permute-start | bytes 14745608 | tf_op jit(solution)/shard_map/cond/branch_18_fun/ppermute | solution.py:153
  132.5 11.4 %slice-start = ((s8[4915200]{0:T(1024)(128)(4,1)}), s8[4194304]{0:T(1024)(128)(4,1)S(1)}, s32[]{:S(2)}) async-start(s8[4915200]{0:T(1024)(128)(4,1)} %bitcast.5), calls=%async_computation | async-start | bytes 8388608
  132.5 11.4 %slice-start.1 = ((s8[4915200]{0:T(1024)(128)(4,1)}), s8[720896]{0:T(1024)(128)(4,1)S(1)}, s32[]{:S(2)}) async-start(s8[4915200]{0:T(1024)(128)(4,1)} %bitcast.5), calls=%async_computation.1 | async-start | bytes 1441792
  139.2 3.6 %collective-permute-start.31 = (f32[256,1024]{1,0:T(8,128)S(1)}, f32[256,1024]{1,0:T(8,128)S(1)}, u32[]{:S(2)}, u32[]{:S(2)}) collective-permute-start(f32[256,1024]{1,0:T(8,128)S(1)} %get-tuple-element.79), channel_id=1, source_target_pairs={{0,32},{32,0},{64,96},{96,64},{1,33},{33,1},{65,97},{97,65},{2,34}... | collective-permute-start | bytes 3145736 | tf_op jit(solution)/shard_map/ppermute | solution.py:158
  143.0 13.2 %collective-permute-start.32 = (bf16[256,1024]{1,0:T(8,128)(2,1)S(1)}, bf16[256,1024]{1,0:T(8,128)(2,1)S(1)}, u32[]{:S(2)}, u32[]{:S(2)}) collective-permute-start(bf16[256,1024]{1,0:T(8,128)(2,1)S(1)} %add_convert_fusion), channel_id=1, source_target_pairs={{0,64},{32,96},{64,0},{96,32},{1,65},{33,97},{65,1},{97,33},{2,66}... | collective-permute-start | bytes 1572872 | tf_op jit(solution)/shard_map/ppermute | solution.py:163
  143.9 14.3 %copy-start.1 = (s32[32]{0:T(128)S(1)}, s32[32]{0:T(128)}, u32[]{:S(2)}) copy-start(s32[32]{0:T(128)} %param.39) | copy-start | bytes 388
  156.2 0.8 copy-start
  157.0 4.2 %collective-permute-start.33 = (f32[256,1024]{1,0:T(8,128)S(1)}, f32[256,1024]{1,0:T(8,128)S(1)}, u32[]{:S(2)}, u32[]{:S(2)}) collective-permute-start(f32[256,1024]{1,0:T(8,128)S(1)} %get-tuple-element.85), channel_id=1, source_target_pairs={{0,32},{32,0},{64,96},{96,64},{1,33},{33,1},{65,97},{97,65},{2,34}... | collective-permute-start | bytes 3145736 | tf_op jit(solution)/shard_map/ppermute | solution.py:158

commit v5 on v4

--- a/solution.py
+++ b/solution.py
@@ -17,7 +17,7 @@
 LIMIT = 60 << 20
 FISHER_LIMIT = 40 << 20
 LANES = 128
-TILE = 512
+TILE = 1024
 STRIP = 256
 
 
@@ -162,14 +162,14 @@
     leaving, place = lax.optimization_barrier((leaving, subj_index))
     far = lax.ppermute(leaving, "subj", [(d, d ^ 2) for d in range(4)])
     near, kept = fisher_sum(arrived, own, place, 0)
-    near, far = lax.optimization_barrier((near, far))
+    block_ids = jnp.arange(block_total, dtype=jnp.int32)
+    own_count = jnp.sum(jnp.where(block_ids == own_block, vertex_count, 0))
+    partner_count = jnp.sum(jnp.where(block_ids == partner, vertex_count, 0))
+    near, far, own_count, partner_count = lax.optimization_barrier((near, far, own_count, partner_count))
     near = to_other_core(near)
     kept, near = lax.optimization_barrier((kept + far.astype(jnp.float32), near))
     summed = kept + near
 
-    block_ids = jnp.arange(block_total, dtype=jnp.int32)
-    own_count = jnp.sum(jnp.where(block_ids == own_block, vertex_count, 0))
-    partner_count = jnp.sum(jnp.where(block_ids == partner, vertex_count, 0))
     row_slots = subj_index * share + jnp.arange(share, dtype=jnp.int32)
     col_slots = jnp.arange(width, dtype=jnp.int32)
     keep_mask = (row_slots < partner_count)[:, None] & (col_slots < own_count)[None, :]

time: 163 us -> 160 us (0.982)
  starting transfers between devices: 11.4 us -> 7.27 us
    ppermute x1, starting transfers between devices: 7.99 us -> 3.05 us  [case(): return lambda value: lax.ppermute(value, 'blk', pairs)]
    ppermute x1, waiting for transfers between devices: 106 us -> 109 us  [case(): return lambda value: lax.ppermute(value, 'blk', pairs)]
    ppermute x1, waiting for transfers between devices: 7.18 us -> 4.62 us  [local(): far = lax.ppermute(leaving, 'subj', [(d, d ^ 2) for d in range(4)])]
  transfers between devices with their start and end apart: 4 -> 4, of which waited for: 3 -> 3; matrix products, arithmetic and copies ran while one was open for 2% -> 2% of each run, Pallas kernels for 3% -> 4%
where the time goes in v5:
time: 160 us; the launch traced here: 159 us
  waiting for transfers between devices  116 us (72%)
  Pallas kernels  30.5 us (19%)
  starting transfers between devices  7.27 us (5%)
  other arithmetic  4.41 us (3%)
    ppermute x1, waiting for transfers between devices, case(): return lambda value: lax.ppermute(value, 'blk', pairs)  109 us
    pallas_call x1, Pallas kernels, normalize(): pl.pallas_call(normalize_kernel, grid=(subjects, width // TILE), in_specs...  17.3 us
    pallas_call x2, Pallas kernels, fisher_sum(): pl.pallas_call(functools.partial(fisher_kernel, frames), grid_spec=pltpu....  13.2 us
    ppermute x1, waiting for transfers between devices, local(): far = lax.ppermute(leaving, 'subj', [(d, d ^ 2) for d in range(4)])  4.62 us
  transfers between devices with their start and end apart: 4, of which 3 were waited for; matrix products, arithmetic and copies ran while one was open for 2% of the time, Pallas kernels for 4%

profile of v5, /device:TPU:1, one launch (start us, length us, event | category | flops | bytes accessed | tf_op | source)
XLA Modules:
  0.0 159.4 jit_solution(1349946340373485886)
XLA Ops:
  0.7 17.3 %normalize.1.own_ref = bf16[2,1200,1024]{2,1,0:T(8,128)(2,1)} custom-call(bf16[2,1200,1024]{2,1,0:T(8,128)(2,1)} %series_ref.1, bf16[2,600,1280]{2,1,0:T(8,128)(2,1)} %constant.41.clone.analysis_ref, bf16[2,600,640]{2,1,0:T(8,128)(2,1)} %constant.42.clone.synthesis_ref, f32[2,600,1]{2,1,0:T(8,128)} %constant.43.clone.gains_ref), custom_call_target="tpu_custom_call" | custom-call | tf_op jit(solution)/shard_map/normalize/pallas_call | solution.py:79
  18.0 111.8 %conditional.1 = (bf16[2,1200,1024]{2,1,0:T(8,128)(2,1)}) conditional(s32[]{:T(128)} %clamp.3, bf16[2,1200,1024]{2,1,0:T(8,128)(2,1)} %normalize.1.own_ref, bf16[2,1200,1024]{2,1,0:T(8,128)(2,1)} %normalize.1.own_ref, bf16[2,1200,1024]{2,1,0:T(8,128)(2,1)} %normalize.1.own_ref, ...), branch_computations={%region_0.1_spmd, %region_1.2_spmd, %region_2.3_spmd, %region_3.4_... | conditional | bytes 19660848 | solution.py:155
  18.0 3.1 %collective-permute-start.9 = (bf16[2,1200,1024]{2,1,0:T(8,128)(2,1)}, bf16[2,1200,1024]{2,1,0:T(8,128)(2,1)}, u32[]{:S(2)}, u32[]{:S(2)}) collective-permute-start(bf16[2,1200,1024]{2,1,0:T(8,128)(2,1)} %param.9), channel_id=1, source_target_pairs={{0,10},{1,11},{2,12},{3,13},{4,14},{5,15},{6,16},{7,17},{8,18},{9,... | collective-permute-start | bytes 14745608 | tf_op jit(solution)/shard_map/cond/branch_9_fun/ppermute | solution.py:153
  21.0 108.8 %collective-permute-done.9 = bf16[2,1200,1024]{2,1,0:T(8,128)(2,1)} collective-permute-done((bf16[2,1200,1024]{2,1,0:T(8,128)(2,1)}, bf16[2,1200,1024]{2,1,0:T(8,128)(2,1)}, u32[]{:S(2)}, u32[]{:S(2)}) %collective-permute-start.9) | collective-permute-done | bytes 4915232 | tf_op jit(solution)/shard_map/cond/branch_9_fun/ppermute | solution.py:153
  129.8 0.0 copy-start.1
  129.8 6.6 %fisher.2 = (f32[256,1024]{1,0:T(8,128)S(1)}, f32[256,1024]{1,0:T(8,128)S(1)}) custom-call(s32[1]{0:T(128)} %bitcast.place_ref, bf16[2,1200,1024]{2,1,0:T(8,128)(2,1)} %get-tuple-element.94.partner_ref, bf16[2,1200,1024]{2,1,0:T(8,128)(2,1)} %normalize.1.own_ref), custom_call_target="tpu_custom_call" | custom-call | flops 1 | bytes 1 | tf_op jit(solution)/shard_map/fisher/pallas_call | solution.py:120
  136.4 1.5 collective-permute-start.31
  137.9 2.3 %collective-permute-done.31 = f32[256,1024]{1,0:T(8,128)S(1)} collective-permute-done((f32[256,1024]{1,0:T(8,128)S(1)}, f32[256,1024]{1,0:T(8,128)S(1)}, u32[]{:S(2)}, u32[]{:S(2)}) %collective-permute-start.31) | collective-permute-done | bytes 1048608 | tf_op jit(solution)/shard_map/ppermute | solution.py:158
  140.2 0.2 add_convert_fusion
  140.3 1.7 %collective-permute-start.32 = (bf16[256,1024]{1,0:T(8,128)(2,1)S(1)}, bf16[256,1024]{1,0:T(8,128)(2,1)S(1)}, u32[]{:S(2)}, u32[]{:S(2)}) collective-permute-start(bf16[256,1024]{1,0:T(8,128)(2,1)S(1)} %add_convert_fusion), channel_id=1, source_target_pairs={{0,64},{32,96},{64,0},{96,32},{1,65},{33,97},{65,1},{97,33},{2,66}... | collective-permute-start | bytes 1572872 | tf_op jit(solution)/shard_map/ppermute | solution.py:163
  142.0 0.0 copy-done.1
  142.0 0.6 fusion.1
  142.7 6.6 %fisher.3 = (f32[256,1024]{1,0:T(8,128)S(1)}, f32[256,1024]{1,0:T(8,128)S(1)}) custom-call(s32[1]{0:T(128)} %bitcast.2.place_ref, bf16[2,1200,1024]{2,1,0:T(8,128)(2,1)} %get-tuple-element.94.partner_ref, bf16[2,1200,1024]{2,1,0:T(8,128)(2,1)} %normalize.1.own_ref), custom_call_target="tpu_custom_call" | custom-call | flops 1 | bytes 1 | tf_op jit(solution)/shard_map/fisher/pallas_call | solution.py:120
  149.3 4.6 %collective-permute-done.32 = bf16[256,1024]{1,0:T(8,128)(2,1)S(1)} collective-permute-done((bf16[256,1024]{1,0:T(8,128)(2,1)S(1)}, bf16[256,1024]{1,0:T(8,128)(2,1)S(1)}, u32[]{:S(2)}, u32[]{:S(2)}) %collective-permute-start.32) | collective-permute-done | bytes 524320 | tf_op jit(solution)/shard_map/ppermute | solution.py:163
  153.9 0.0 copy-start
  153.9 0.8 copy-done
  154.7 1.0 collective-permute-start.33
  155.7 0.6 add_compare_fusion
  156.3 0.6 iota_compare_fusion
  156.9 1.2 convert_add_fusion
  158.1 0.0 collective-permute-done.33
  158.1 1.2 multiply_select_fusion
Async XLA Ops:
  18.0 111.8 %collective-permute-start.9 = (bf16[2,1200,1024]{2,1,0:T(8,128)(2,1)}, bf16[2,1200,1024]{2,1,0:T(8,128)(2,1)}, u32[]{:S(2)}, u32[]{:S(2)}) collective-permute-start(bf16[2,1200,1024]{2,1,0:T(8,128)(2,1)} %param.9), channel_id=1, source_target_pairs={{0,10},{1,11},{2,12},{3,13},{4,14},{5,15},{6,16},{7,17},{8,18},{9,... | collective-permute-start | bytes 14745608 | tf_op jit(solution)/shard_map/cond/branch_9_fun/ppermute | solution.py:153
  129.8 12.3 %copy-start.1 = (s32[32]{0:T(128)S(1)}, s32[32]{0:T(128)}, u32[]{:S(2)}) copy-start(s32[32]{0:T(128)} %param.39) | copy-start | bytes 388
  136.4 3.8 %collective-permute-start.31 = (f32[256,1024]{1,0:T(8,128)S(1)}, f32[256,1024]{1,0:T(8,128)S(1)}, u32[]{:S(2)}, u32[]{:S(2)}) collective-permute-start(f32[256,1024]{1,0:T(8,128)S(1)} %get-tuple-element.81), channel_id=1, source_target_pairs={{0,32},{32,0},{64,96},{96,64},{1,33},{33,1},{65,97},{97,65},{2,34}... | collective-permute-start | bytes 3145736 | tf_op jit(solution)/shard_map/ppermute | solution.py:158
  140.3 13.6 %collective-permute-start.32 = (bf16[256,1024]{1,0:T(8,128)(2,1)S(1)}, bf16[256,1024]{1,0:T(8,128)(2,1)S(1)}, u32[]{:S(2)}, u32[]{:S(2)}) collective-permute-start(bf16[256,1024]{1,0:T(8,128)(2,1)S(1)} %add_convert_fusion), channel_id=1, source_target_pairs={{0,64},{32,96},{64,0},{96,32},{1,65},{33,97},{65,1},{97,33},{2,66}... | collective-permute-start | bytes 1572872 | tf_op jit(solution)/shard_map/ppermute | solution.py:163
  153.9 0.8 copy-start
  154.7 3.4 %collective-permute-start.33 = (f32[256,1024]{1,0:T(8,128)S(1)}, f32[256,1024]{1,0:T(8,128)S(1)}, u32[]{:S(2)}, u32[]{:S(2)}) collective-permute-start(f32[256,1024]{1,0:T(8,128)S(1)} %get-tuple-element.89), channel_id=1, source_target_pairs={{0,32},{32,0},{64,96},{96,64},{1,33},{33,1},{65,97},{97,65},{2,34}... | collective-permute-start | bytes 3145736 | tf_op jit(solution)/shard_map/ppermute | solution.py:158
